TPU v7x, 512 devices: a whole 4x8x8 slice. The times are simulated.
512 devices in a mesh: blk: 128 (over x, z_lo, y, core), rows: 4 (over z_hi).
Axes of the slice: x: 4, y: 8, z: 8 (z_hi: 4, z_lo: 2; z = z_hi * 2 + z_lo), core: 2. Of those that a mesh axis runs over, the one named last changes fastest.
Arguments:
- weight: bfloat16 [1024, 16384], P('blk', 'rows')
- factor: bfloat16 [16384, 16384], P('rows', 'blk')
- pairing: int32 [4, 64], replicated, may hold values from 0 to 63, each once within a row
Outputs:
- rotated: float32 [1024, 16384], P('rows', 'blk')
- right_factor: float32 [16384, 16384], P('rows', 'blk')
Inputs may be any that keep to these rules, and one draw needn't show every extreme that they name: Each row of pairing lists every column index of a block once.
All inputs are finite; a program needn't handle non-finite values.
Results may differ from a plain program's by a relative error of at most 0.0003.
Values may be sent and summed in bfloat16 or wider, within the bound.
A program may use at most 64 MiB of HBM per device.

v0:
```python
import jax
import jax.numpy as jnp
from jax import lax
from jax.sharding import PartitionSpec as P

BLOCK = 64
STEPS = 4


def shifted(x, axis, by):
    count = lax.axis_size(axis)
    return lax.ppermute(x, axis, [(i, (i + by) % count) for i in range(count)])


def turn_pair(upper_cols, lower_cols, upper_factor, lower_factor, pair_order):
    columns = pair_order.shape[0]
    ladder = lax.broadcasted_iota(jnp.int32, (columns, columns), 0)
    targets = lax.broadcasted_iota(jnp.int32, (columns, columns), 1)
    matches = (pair_order[:, None] == targets).astype(jnp.int32)
    inverse = jnp.sum(matches * ladder, axis=0)
    partner = jnp.take(lower_cols, pair_order, axis=0)
    partner_factor = jnp.take(lower_factor, pair_order, axis=0)
    upper_norm = jnp.sum(upper_cols * upper_cols, axis=1)
    lower_norm = jnp.sum(partner * partner, axis=1)
    cross_term = jnp.sum(upper_cols * partner, axis=1)
    upper_norm, lower_norm, cross_term = lax.psum((upper_norm, lower_norm, cross_term), "rows")
    rotation_angle = 0.5 * jnp.arctan2(2.0 * cross_term, upper_norm - lower_norm)
    cosine = jnp.cos(rotation_angle)[:, None]
    sine_part = jnp.sin(rotation_angle)[:, None]
    new_upper = cosine * upper_cols + sine_part * partner
    new_partner = cosine * partner - sine_part * upper_cols
    new_upper_factor = cosine * upper_factor + sine_part * partner_factor
    new_partner_factor = cosine * partner_factor - sine_part * upper_factor
    return (
        new_upper,
        jnp.take(new_partner, inverse, axis=0),
        new_upper_factor,
        jnp.take(new_partner_factor, inverse, axis=0),
    )


def per_device(weight, factor, pairing):
    partial_cols = lax.dot_general(
        factor,
        lax.all_gather(weight, "blk", axis=0, tiled=True),
        (((0,), (1,)), ((), ())),
        preferred_element_type=jnp.float32,
    )
    whitened = lax.psum_scatter(partial_cols, "rows", scatter_dimension=1, tiled=True)
    upper_cols = whitened[:BLOCK, :]
    lower_cols = whitened[BLOCK:, :]
    right_cols = factor.astype(jnp.float32).T
    upper_factor = right_cols[:BLOCK, :]
    lower_factor = right_cols[BLOCK:, :]
    for step_index in range(STEPS):
        if step_index > 0:
            upper_cols, upper_factor = shifted((upper_cols, upper_factor), "blk", 1)
            lower_cols, lower_factor = shifted((lower_cols, lower_factor), "blk", -1)
        upper_cols, lower_cols, upper_factor, lower_factor = turn_pair(
            upper_cols, lower_cols, upper_factor, lower_factor, pairing[step_index]
        )
    rotated = jnp.concatenate([upper_cols, lower_cols], axis=0)
    right_factor = jnp.concatenate([upper_factor, lower_factor], axis=0)
    return (rotated.T, right_factor.T)


def solution(mesh):
    in_specs = (P("blk", "rows"), P("rows", "blk"), P())
    out_specs = (P("rows", "blk"), P("rows", "blk"))
    return jax.shard_map(
        per_device, mesh=mesh, in_specs=in_specs, out_specs=out_specs, check_vma=False
    )
```

profile of v0, /device:TPU:128, one launch (start us, length us, event | category | flops | bytes accessed | tf_op | source)
XLA Modules:
  0.0 416.7 jit_solution(13958710799210260204)
XLA Ops:
  7.2 0.7 all-gather.2.cloned.1.call-update
  8.0 2.3 copy.8
  10.6 1.4 convert_bitcast_fusion
  12.0 223.4 %all-gather.2.cloned.1.call-done = bf16[1024,4096]{1,0:T(8,128)(2,1)} async-done(((bf16[8,4096]{1,0:T(8,128)(2,1)}), bf16[1024,4096]{1,0:T(8,128)(2,1)}) %all-gather.2.cloned.1.call-update) | async-done | bytes 8388624 | tf_op jit(solution)/shard_map/all_gather | solution.py:45
  235.5 7.1 %fusion.4 = f32[128,1024]{1,0:T(8,128)} fusion(bf16[4096,128]{1,0:T(8,128)(2,1)S(1)} %copy-done, bf16[1024,4096]{1,0:T(8,128)(2,1)} %all-gather.2.cloned.1.call-done), kind=kOutput, calls=%fused_computation.99 | convolution fusion | flops 1073741824 | bytes 9961472 | tf_op jit(solution)/shard_map/dot_general | solution.py:43
  242.7 1.8 gather_fusion.8
  244.7 28.6 %reduce-scatter.2.cloned.1.call-done = f32[128,256]{1,0:T(8,128)} async-done(((f32[128,1024]{1,0:T(8,128)}), f32[128,256]{1,0:T(8,128)}) %reduce-scatter.2.cloned.1.call-update) | async-done | bytes 131088 | tf_op jit(solution)/shard_map/reduce_scatter | solution.py:49
  273.3 0.8 slice.65
  274.8 1.1 multiply_reduce_fusion.11
  275.9 9.7 %all-reduce.3 = (f32[64]{0:T(128)S(1)}, f32[64]{0:T(128)S(1)}, f32[64]{0:T(128)S(1)}) all-reduce(f32[64]{0:T(128)S(1)} %get-tuple-element.9, f32[64]{0:T(128)S(1)} %get-tuple-element.16, f32[64]{0:T(128)S(1)} %get-tuple-element.8), channel_id=1, replica_groups=mesh['blk'=128,'rows'=4] {'rows'}, use_global_device_ids=true, to_apply=%region_4.6 | all-reduce | flops 192 | bytes 1536 | tf_op jit(solution)/shard_map/psum | solution.py:26
  285.7 2.5 multiply_subtract_fusion.3
  288.3 0.9 gather_fusion.9
  289.2 1.2 broadcast_select_fusion.3
  290.4 2.8 collective-permute-start.7
  293.2 1.9 collective-permute-start.6
  296.0 7.9 %collective-permute-start.1 = (f32[64,256]{1,0:T(8,128)S(1)}, f32[64,256]{1,0:T(8,128)S(1)}, u32[]{:S(2)}, u32[]{:S(2)}) collective-permute-start(f32[64,256]{1,0:T(8,128)S(1)} %broadcast_select_fusion.7), channel_id=1, source_target_pairs={{0,508},{4,0},{8,4},{12,8},{16,12},{20,16},{24,20},{28,24},{32,28}... | collective-permute-start | bytes 196616 | tf_op jit(solution)/shard_map/ppermute | solution.py:12
  303.9 1.9 collective-permute-start
  307.1 7.2 %collective-permute-done = f32[64,256]{1,0:T(8,128)S(1)} collective-permute-done((f32[64,256]{1,0:T(8,128)S(1)}, f32[64,256]{1,0:T(8,128)S(1)}, u32[]{:S(2)}, u32[]{:S(2)}) %collective-permute-start) | collective-permute-done | bytes 65568 | tf_op jit(solution)/shard_map/ppermute | solution.py:12
  314.5 11.2 %all-reduce.2 = (f32[64]{0:T(128)S(1)}, f32[64]{0:T(128)S(1)}, f32[64]{0:T(128)S(1)}) all-reduce(f32[64]{0:T(128)S(1)} %get-tuple-element.19, f32[64]{0:T(128)S(1)} %get-tuple-element.15, f32[64]{0:T(128)S(1)} %get-tuple-element.14), channel_id=1, replica_groups=mesh['blk'=128,'rows'=4] {'rows'}, use_global_device_ids=true, to_apply=%region_11.13 | all-reduce | flops 192 | bytes 1536 | tf_op jit(solution)/shard_map/psum | solution.py:26
  325.8 0.9 gather_fusion.10
  326.7 1.6 multiply_subtract_fusion.2
  328.3 0.9 gather_fusion.11
  329.2 1.1 broadcast_select_fusion.2
  330.3 1.9 collective-permute-start.9
  332.3 2.4 collective-permute-start.8
  334.8 0.7 gather_fusion.3
  335.5 7.4 %collective-permute-start.3 = (f32[64,256]{1,0:T(8,128)S(1)}, f32[64,256]{1,0:T(8,128)S(1)}, u32[]{:S(2)}, u32[]{:S(2)}) collective-permute-start(f32[64,256]{1,0:T(8,128)S(1)} %broadcast_select_fusion.6), channel_id=1, source_target_pairs={{0,508},{4,0},{8,4},{12,8},{16,12},{20,16},{24,20},{28,24},{32,28}... | collective-permute-start | bytes 196616 | tf_op jit(solution)/shard_map/ppermute | solution.py:12
  342.9 1.9 collective-permute-start.2
  346.1 7.2 %collective-permute-done.2 = f32[64,256]{1,0:T(8,128)S(1)} collective-permute-done((f32[64,256]{1,0:T(8,128)S(1)}, f32[64,256]{1,0:T(8,128)S(1)}, u32[]{:S(2)}, u32[]{:S(2)}) %collective-permute-start.2) | collective-permute-done | bytes 65568 | tf_op jit(solution)/shard_map/ppermute | solution.py:12
  353.6 9.9 %all-reduce.1 = (f32[64]{0:T(128)S(1)}, f32[64]{0:T(128)S(1)}, f32[64]{0:T(128)S(1)}) all-reduce(f32[64]{0:T(128)S(1)} %get-tuple-element.18, f32[64]{0:T(128)S(1)} %get-tuple-element.13, f32[64]{0:T(128)S(1)} %get-tuple-element.12), channel_id=1, replica_groups=mesh['blk'=128,'rows'=4] {'rows'}, use_global_device_ids=true, to_apply=%region_18.20 | all-reduce | flops 192 | bytes 1536 | tf_op jit(solution)/shard_map/psum | solution.py:26
  363.7 0.7 gather_fusion.5
  364.4 0.9 gather_fusion.12
  365.4 1.6 multiply_subtract_fusion.1
  366.9 0.9 gather_fusion.13
  367.9 1.1 broadcast_select_fusion.1
  369.0 1.9 collective-permute-start.11
  370.9 2.4 collective-permute-start.10
  373.4 7.4 %collective-permute-start.5 = (f32[64,256]{1,0:T(8,128)S(1)}, f32[64,256]{1,0:T(8,128)S(1)}, u32[]{:S(2)}, u32[]{:S(2)}) collective-permute-start(f32[64,256]{1,0:T(8,128)S(1)} %broadcast_select_fusion.5), channel_id=1, source_target_pairs={{0,508},{4,0},{8,4},{12,8},{16,12},{20,16},{24,20},{28,24},{32,28}... | collective-permute-start | bytes 196616 | tf_op jit(solution)/shard_map/ppermute | solution.py:12
  380.8 1.9 collective-permute-start.4
  382.7 1.4 collective-permute-done.5
  384.8 7.3 %collective-permute-done.4 = f32[64,256]{1,0:T(8,128)S(1)} collective-permute-done((f32[64,256]{1,0:T(8,128)S(1)}, f32[64,256]{1,0:T(8,128)S(1)}, u32[]{:S(2)}, u32[]{:S(2)}) %collective-permute-start.4) | collective-permute-done | bytes 65568 | tf_op jit(solution)/shard_map/ppermute | solution.py:12
  392.2 10.3 %all-reduce = (f32[64]{0:T(128)S(1)}, f32[64]{0:T(128)S(1)}, f32[64]{0:T(128)S(1)}) all-reduce(f32[64]{0:T(128)S(1)} %get-tuple-element.17, f32[64]{0:T(128)S(1)} %get-tuple-element.11, f32[64]{0:T(128)S(1)} %get-tuple-element.10), channel_id=1, replica_groups=mesh['blk'=128,'rows'=4] {'rows'}, use_global_device_ids=true, to_apply=%region_25.27 | all-reduce | flops 192 | bytes 1536 | tf_op jit(solution)/shard_map/psum | solution.py:26
  402.8 0.7 gather_fusion.7
  403.5 0.8 copy.9
  404.3 0.9 gather_fusion.14
  405.2 1.6 multiply_add_fusion
  406.8 0.9 gather_fusion.15
  408.0 1.8 copy.10
  (69 shorter events, 7.3 us)
Async XLA Ops:
  7.2 3.1 copy-start.3
  7.2 228.3 %all-gather.2.cloned.1.call-start = ((), (), s32[]{:S(2)}) async-start(), calls=%async_computation.1 | async-start | bytes 8454144 | tf_op jit(solution)/shard_map/all_gather | solution.py:45
  7.9 265.4 %reduce-scatter.2.cloned.1.call-start = ((), (), s32[]{:S(2)}) async-start(), calls=%async_computation.2 | async-start | bytes 655360 | tf_op jit(solution)/shard_map/reduce_scatter | solution.py:49
  10.2 225.2 %copy-start = (bf16[4096,128]{1,0:T(8,128)(2,1)S(1)}, bf16[4096,128]{1,0:T(8,128)(2,1)}, u32[]{:S(2)}) copy-start(bf16[4096,128]{1,0:T(8,128)(2,1)} %param.8) | copy-start | bytes 3145732
  289.2 4.0 copy-start.1
  289.2 6.0 %copy-start.2 = (f32[128,256]{1,0:T(8,128)S(1)}, f32[128,256]{1,0:T(8,128)}, u32[]{:S(2)}) copy-start(f32[128,256]{1,0:T(8,128)} %reduce-scatter.2.cloned.1.call-done) | copy-start | bytes 393220
  290.4 35.4 %collective-permute-start.7 = (f32[64,4096]{1,0:T(8,128)}, f32[64,4096]{1,0:T(8,128)S(1)}, u32[]{:S(2)}, u32[]{:S(2)}) collective-permute-start(f32[64,4096]{1,0:T(8,128)} %broadcast_select_fusion.3), channel_id=1, source_target_pairs={{0,508},{4,0},{8,4},{12,8},{16,12},{20,16},{24,20},{28,24},{32,28}... | collective-permute-start | bytes 3145736 | tf_op jit(solution)/shard_map/ppermute | solution.py:12
  293.2 33.5 %collective-permute-start.6 = (f32[64,4096]{1,0:T(8,128)S(1)}, f32[64,4096]{1,0:T(8,128)}, u32[]{:S(2)}, u32[]{:S(2)}) collective-permute-start(f32[64,4096]{1,0:T(8,128)S(1)} %copy-done.1), channel_id=1, source_target_pairs={{0,4},{4,8},{8,12},{12,16},{16,20},{20,24},{24,28},{28,32},{32,36}... | collective-permute-start | bytes 3145736 | tf_op jit(solution)/shard_map/ppermute | solution.py:12
  296.0 10.4 %collective-permute-start.1 = (f32[64,256]{1,0:T(8,128)S(1)}, f32[64,256]{1,0:T(8,128)S(1)}, u32[]{:S(2)}, u32[]{:S(2)}) collective-permute-start(f32[64,256]{1,0:T(8,128)S(1)} %broadcast_select_fusion.7), channel_id=1, source_target_pairs={{0,508},{4,0},{8,4},{12,8},{16,12},{20,16},{24,20},{28,24},{32,28}... | collective-permute-start | bytes 196616 | tf_op jit(solution)/shard_map/ppermute | solution.py:12
  303.9 10.4 %collective-permute-start = (f32[64,256]{1,0:T(8,128)S(1)}, f32[64,256]{1,0:T(8,128)S(1)}, u32[]{:S(2)}, u32[]{:S(2)}) collective-permute-start(f32[64,256]{1,0:T(8,128)S(1)} %get-tuple-element.57), channel_id=1, source_target_pairs={{0,4},{4,8},{8,12},{12,16},{16,20},{20,24},{24,28},{28,32},{32,36}... | collective-permute-start | bytes 196616 | tf_op jit(solution)/shard_map/ppermute | solution.py:12
  330.3 34.1 %collective-permute-start.9 = (f32[64,4096]{1,0:T(8,128)}, f32[64,4096]{1,0:T(8,128)S(1)}, u32[]{:S(2)}, u32[]{:S(2)}) collective-permute-start(f32[64,4096]{1,0:T(8,128)} %broadcast_select_fusion.2), channel_id=1, source_target_pairs={{0,508},{4,0},{8,4},{12,8},{16,12},{20,16},{24,20},{28,24},{32,28}... | collective-permute-start | bytes 3145736 | tf_op jit(solution)/shard_map/ppermute | solution.py:12
  332.3 33.1 %collective-permute-start.8 = (f32[64,4096]{1,0:T(8,128)S(1)}, f32[64,4096]{1,0:T(8,128)}, u32[]{:S(2)}, u32[]{:S(2)}) collective-permute-start(f32[64,4096]{1,0:T(8,128)S(1)} %get-tuple-element.55), channel_id=1, source_target_pairs={{0,4},{4,8},{8,12},{12,16},{16,20},{20,24},{24,28},{28,32},{32,36}... | collective-permute-start | bytes 3145736 | tf_op jit(solution)/shard_map/ppermute | solution.py:12
  335.5 10.0 %collective-permute-start.3 = (f32[64,256]{1,0:T(8,128)S(1)}, f32[64,256]{1,0:T(8,128)S(1)}, u32[]{:S(2)}, u32[]{:S(2)}) collective-permute-start(f32[64,256]{1,0:T(8,128)S(1)} %broadcast_select_fusion.6), channel_id=1, source_target_pairs={{0,508},{4,0},{8,4},{12,8},{16,12},{20,16},{24,20},{28,24},{32,28}... | collective-permute-start | bytes 196616 | tf_op jit(solution)/shard_map/ppermute | solution.py:12
  342.9 10.5 %collective-permute-start.2 = (f32[64,256]{1,0:T(8,128)S(1)}, f32[64,256]{1,0:T(8,128)S(1)}, u32[]{:S(2)}, u32[]{:S(2)}) collective-permute-start(f32[64,256]{1,0:T(8,128)S(1)} %get-tuple-element.63), channel_id=1, source_target_pairs={{0,4},{4,8},{8,12},{12,16},{16,20},{20,24},{24,28},{28,32},{32,36}... | collective-permute-start | bytes 196616 | tf_op jit(solution)/shard_map/ppermute | solution.py:12
  369.0 35.3 %collective-permute-start.11 = (f32[64,4096]{1,0:T(8,128)}, f32[64,4096]{1,0:T(8,128)S(1)}, u32[]{:S(2)}, u32[]{:S(2)}) collective-permute-start(f32[64,4096]{1,0:T(8,128)} %broadcast_select_fusion.1), channel_id=1, source_target_pairs={{0,508},{4,0},{8,4},{12,8},{16,12},{20,16},{24,20},{28,24},{32,28}... | collective-permute-start | bytes 3145736 | tf_op jit(solution)/shard_map/ppermute | solution.py:12
  370.9 34.3 %collective-permute-start.10 = (f32[64,4096]{1,0:T(8,128)S(1)}, f32[64,4096]{1,0:T(8,128)}, u32[]{:S(2)}, u32[]{:S(2)}) collective-permute-start(f32[64,4096]{1,0:T(8,128)S(1)} %get-tuple-element.53), channel_id=1, source_target_pairs={{0,4},{4,8},{8,12},{12,16},{16,20},{20,24},{24,28},{28,32},{32,36}... | collective-permute-start | bytes 3145736 | tf_op jit(solution)/shard_map/ppermute | solution.py:12
  373.4 10.7 %collective-permute-start.5 = (f32[64,256]{1,0:T(8,128)S(1)}, f32[64,256]{1,0:T(8,128)S(1)}, u32[]{:S(2)}, u32[]{:S(2)}) collective-permute-start(f32[64,256]{1,0:T(8,128)S(1)} %broadcast_select_fusion.5), channel_id=1, source_target_pairs={{0,508},{4,0},{8,4},{12,8},{16,12},{20,16},{24,20},{28,24},{32,28}... | collective-permute-start | bytes 196616 | tf_op jit(solution)/shard_map/ppermute | solution.py:12
  380.8 11.3 %collective-permute-start.4 = (f32[64,256]{1,0:T(8,128)S(1)}, f32[64,256]{1,0:T(8,128)S(1)}, u32[]{:S(2)}, u32[]{:S(2)}) collective-permute-start(f32[64,256]{1,0:T(8,128)S(1)} %get-tuple-element.61), channel_id=1, source_target_pairs={{0,4},{4,8},{8,12},{12,16},{16,20},{20,24},{24,28},{28,32},{32,36}... | collective-permute-start | bytes 196616 | tf_op jit(solution)/shard_map/ppermute | solution.py:12
Sparse Core Ops, SparseCore 0:
  10.2 225.2 all-gather.1
  242.8 30.5 reduce-scatter.1
where the time goes:
time: 417 us
  waiting for transfers between devices  277 us (66%)
  starting transfers between devices  41.8 us (10%)
  blocking collectives  41.1 us (10%)
  local copies, waits for them, and re-layouts  19.5 us (5%)
  other arithmetic  15.6 us (4%)
  between operations  14.5 us (3%)
  matrix products  7.14 us (2%)
    all_gather x1, waiting for transfers between devices, per_device(): lax.all_gather(weight, 'blk', axis=0, tiled=True)  223 us
    ppermute x12, starting transfers between devices, shifted(): return lax.ppermute(x, axis, [(i, (i + by) % count) for i in range(count)])  41.7 us
    psum x4, blocking collectives, turn_pair(): lax.psum((upper_norm, lower_norm, cross_term), 'rows')  41.1 us
    reduce_scatter x1, waiting for transfers between devices, per_device(): lax.psum_scatter(partial_cols, 'rows', scatter_dimension=1, tiled=True)  28.6 us
    ppermute x12, waiting for transfers between devices, shifted(): return lax.ppermute(x, axis, [(i, (i + by) % count) for i in range(count)])  24.3 us
  transfers between devices with their start and end apart: 14, of which 8 were waited for; matrix products, arithmetic and copies ran while one was open for 4% of the time, Pallas kernels for 0%

commit v1 on v0

--- a/solution.py
+++ b/solution.py
@@ -5,6 +5,18 @@
 
 BLOCK = 64
 STEPS = 4
+
+
+def update_counts(local_x):
+    return jnp.concatenate(
+        lax.all_to_all(
+            jnp.stack([local_x for _ in range(lax.axis_size("blk"))], 0),
+            "blk",
+            split_axis=0,
+            concat_axis=0,
+        ),
+        0,
+    )
 
 
 def shifted(x, axis, by):
@@ -41,10 +53,7 @@
 
 def per_device(weight, factor, pairing):
     partial_cols = lax.dot_general(
-        factor,
-        lax.all_gather(weight, "blk", axis=0, tiled=True),
-        (((0,), (1,)), ((), ())),
-        preferred_element_type=jnp.float32,
+        factor, update_counts(weight), (((0,), (1,)), ((), ())), preferred_element_type=jnp.float32
     )
     whitened = lax.psum_scatter(partial_cols, "rows", scatter_dimension=1, tiled=True)
     upper_cols = whitened[:BLOCK, :]

time: 417 us -> 394 us (0.945)
  waiting for transfers between devices: 277 us -> 224 us
  starting transfers between devices: 41.8 us -> 67.7 us
    all_gather x1 -> x0, waiting for transfers between devices: 223 us -> none  [per_device(): lax.all_gather(weight, 'blk', axis=0, tiled=True)]
    all_to_all x0 -> x1, waiting for transfers between devices: none -> 183 us  [update_counts(): lax.all_to_all(jnp.stack([local_x for _ in range(lax.axis_size('blk'))],...]
    all_to_all x0 -> x1, starting transfers between devices: none -> 14.3 us  [update_counts(): lax.all_to_all(jnp.stack([local_x for _ in range(lax.axis_size('blk'))],...]
    ppermute x12, starting transfers between devices: 41.7 us -> 53.3 us  [shifted(): return lax.ppermute(x, axis, [(i, (i + by) % count) for i in range(count)])]
    ppermute x12, waiting for transfers between devices: 24.3 us -> 15.2 us  [shifted(): return lax.ppermute(x, axis, [(i, (i + by) % count) for i in range(count)])]
    another operation x0 -> x1, local copies, waits for them, and re-layouts: none -> 5.09 us  [update_counts(): jnp.stack([local_x for _ in range(lax.axis_size('blk'))], 0)]
  transfers between devices with their start and end apart: 14 -> 14, of which waited for: 8 -> 5; matrix products, arithmetic and copies ran while one was open for 4% -> 5% of each run, Pallas kernels for 0% -> 0%
where the time goes in v1:
time: 394 us; the launch traced here: 393 us
  waiting for transfers between devices  224 us (57%)
  starting transfers between devices  67.7 us (17%)
  blocking collectives  41.6 us (11%)
  local copies, waits for them, and re-layouts  23.6 us (6%)
  between operations  14.6 us (4%)
  other arithmetic  14.3 us (4%)
  matrix products  7.14 us (2%)
    all_to_all x1, waiting for transfers between devices, update_counts(): lax.all_to_all(jnp.stack([local_x for _ in range(lax.axis_size('blk'))],...  183 us
    ppermute x12, starting transfers between devices, shifted(): return lax.ppermute(x, axis, [(i, (i + by) % count) for i in range(count)])  53.3 us
    psum x4, blocking collectives, turn_pair(): lax.psum((upper_norm, lower_norm, cross_term), 'rows')  41.6 us
    reduce_scatter x1, waiting for transfers between devices, per_device(): lax.psum_scatter(partial_cols, 'rows', scatter_dimension=1, tiled=True)  26.2 us
    ppermute x12, waiting for transfers between devices, shifted(): return lax.ppermute(x, axis, [(i, (i + by) % count) for i in range(count)])  15.2 us
    all_to_all x1, starting transfers between devices, update_counts(): lax.all_to_all(jnp.stack([local_x for _ in range(lax.axis_size('blk'))],...  14.3 us
  transfers between devices with their start and end apart: 14, of which 5 were waited for; matrix products, arithmetic and copies ran while one was open for 5% of the time, Pallas kernels for 0%

profile of v1, /device:TPU:128, one launch (start us, length us, event | category | flops | bytes accessed | tf_op | source)
XLA Modules:
  0.0 393.3 jit_solution(16112007846726537673)
XLA Ops:
  7.2 5.1 %stack.2 = bf16[128,8,4096]{2,1,0:T(8,128)(2,1)} broadcast(bf16[8,4096]{1,0:T(8,128)(2,1)} %param.7), dimensions={1,2} | broadcast | bytes 8454144 | tf_op jit(solution)/shard_map/stack | solution.py:13
  12.3 14.3 %all-to-all-start = ((bf16[128,8,4096]{2,1,0:T(8,128)(2,1)}), bf16[128,8,4096]{2,1,0:T(8,128)(2,1)}, u32[]{:S(2)}, u32[]{:S(2)}) async-start(bf16[128,8,4096]{2,1,0:T(8,128)(2,1)} %stack.2), calls=%async_computation | async-start | bytes 16777216 | tf_op jit(solution)/shard_map/all_to_all | solution.py:12
  26.6 1.3 copy.8
  28.3 1.4 convert_bitcast_fusion
  29.7 183.0 %all-to-all-done = bf16[128,8,4096]{2,1,0:T(8,128)(2,1)} async-done(((bf16[128,8,4096]{2,1,0:T(8,128)(2,1)}), bf16[128,8,4096]{2,1,0:T(8,128)(2,1)}, u32[]{:S(2)}, u32[]{:S(2)}) %all-to-all-start) | async-done | bytes 8388640 | tf_op jit(solution)/shard_map/all_to_all | solution.py:12
  212.7 7.1 %fusion = f32[128,1024]{1,0:T(8,128)} fusion(bf16[4096,128]{1,0:T(8,128)(2,1)S(1)} %copy-done, bf16[128,8,4096]{2,1,0:T(8,128)(2,1)} %all-to-all-done), kind=kOutput, calls=%fused_computation.16 | convolution fusion | flops 1073741824 | bytes 9961472 | tf_op jit(solution)/shard_map/dot_general | solution.py:55
  220.0 1.8 gather_fusion.8
  221.9 26.2 %reduce-scatter.2.cloned.1.call-done = f32[128,256]{1,0:T(8,128)} async-done(((f32[128,1024]{1,0:T(8,128)}), f32[128,256]{1,0:T(8,128)}) %reduce-scatter.2.cloned.1.call-update) | async-done | bytes 131088 | tf_op jit(solution)/shard_map/reduce_scatter | solution.py:58
  248.2 0.8 slice.65
  249.0 0.7 gather_fusion
  249.7 1.1 multiply_reduce_fusion.11
  250.7 9.6 %all-reduce.3 = (f32[64]{0:T(128)S(1)}, f32[64]{0:T(128)S(1)}, f32[64]{0:T(128)S(1)}) all-reduce(f32[64]{0:T(128)S(1)} %get-tuple-element.9, f32[64]{0:T(128)S(1)} %get-tuple-element.16, f32[64]{0:T(128)S(1)} %get-tuple-element.8), channel_id=1, replica_groups=mesh['blk'=128,'rows'=4] {'rows'}, use_global_device_ids=true, to_apply=%region_4.6 | all-reduce | flops 192 | bytes 1536 | tf_op jit(solution)/shard_map/psum | solution.py:38
  260.4 2.5 multiply_subtract_fusion.3
  262.9 1.9 collective-permute-start.6
  264.9 0.9 gather_fusion.9
  266.0 7.9 %collective-permute-start.7 = (f32[64,4096]{1,0:T(8,128)S(1)}, f32[64,4096]{1,0:T(8,128)S(1)}, u32[]{:S(2)}, u32[]{:S(2)}) collective-permute-start(f32[64,4096]{1,0:T(8,128)S(1)} %broadcast_select_fusion.3), channel_id=1, source_target_pairs={{0,508},{4,0},{8,4},{12,8},{16,12},{20,16},{24,20},{28,24},{32,28}... | collective-permute-start | bytes 3145736 | tf_op jit(solution)/shard_map/ppermute | solution.py:24
  274.0 1.9 collective-permute-start
  275.9 0.7 gather_fusion.1
  276.6 7.9 %collective-permute-start.1 = (f32[64,256]{1,0:T(8,128)S(1)}, f32[64,256]{1,0:T(8,128)S(1)}, u32[]{:S(2)}, u32[]{:S(2)}) collective-permute-start(f32[64,256]{1,0:T(8,128)S(1)} %broadcast_select_fusion.7), channel_id=1, source_target_pairs={{0,508},{4,0},{8,4},{12,8},{16,12},{20,16},{24,20},{28,24},{32,28}... | collective-permute-start | bytes 196616 | tf_op jit(solution)/shard_map/ppermute | solution.py:24
  284.5 2.3 collective-permute-done.1
  287.7 11.6 %all-reduce.2 = (f32[64]{0:T(128)S(1)}, f32[64]{0:T(128)S(1)}, f32[64]{0:T(128)S(1)}) all-reduce(f32[64]{0:T(128)S(1)} %get-tuple-element.19, f32[64]{0:T(128)S(1)} %get-tuple-element.15, f32[64]{0:T(128)S(1)} %get-tuple-element.14), channel_id=1, replica_groups=mesh['blk'=128,'rows'=4] {'rows'}, use_global_device_ids=true, to_apply=%region_11.13 | all-reduce | flops 192 | bytes 1536 | tf_op jit(solution)/shard_map/psum | solution.py:38
  299.5 0.9 gather_fusion.10
  300.4 2.5 multiply_subtract_fusion.2
  302.9 1.9 collective-permute-start.8
  304.9 0.9 gather_fusion.11
  305.8 1.1 broadcast_select_fusion.2
  306.9 7.8 %collective-permute-start.9 = (f32[64,4096]{1,0:T(8,128)}, f32[64,4096]{1,0:T(8,128)S(1)}, u32[]{:S(2)}, u32[]{:S(2)}) collective-permute-start(f32[64,4096]{1,0:T(8,128)} %broadcast_select_fusion.2), channel_id=1, source_target_pairs={{0,508},{4,0},{8,4},{12,8},{16,12},{20,16},{24,20},{28,24},{32,28}... | collective-permute-start | bytes 3145736 | tf_op jit(solution)/shard_map/ppermute | solution.py:24
  314.9 1.9 collective-permute-start.2
  316.8 0.7 gather_fusion.3
  317.6 7.9 %collective-permute-start.3 = (f32[64,256]{1,0:T(8,128)S(1)}, f32[64,256]{1,0:T(8,128)S(1)}, u32[]{:S(2)}, u32[]{:S(2)}) collective-permute-start(f32[64,256]{1,0:T(8,128)S(1)} %broadcast_select_fusion.6), channel_id=1, source_target_pairs={{0,508},{4,0},{8,4},{12,8},{16,12},{20,16},{24,20},{28,24},{32,28}... | collective-permute-start | bytes 196616 | tf_op jit(solution)/shard_map/ppermute | solution.py:24
  325.4 2.6 collective-permute-done.3
  328.9 8.6 %all-reduce.1 = (f32[64]{0:T(128)S(1)}, f32[64]{0:T(128)S(1)}, f32[64]{0:T(128)S(1)}) all-reduce(f32[64]{0:T(128)S(1)} %get-tuple-element.18, f32[64]{0:T(128)S(1)} %get-tuple-element.13, f32[64]{0:T(128)S(1)} %get-tuple-element.12), channel_id=1, replica_groups=mesh['blk'=128,'rows'=4] {'rows'}, use_global_device_ids=true, to_apply=%region_18.20 | all-reduce | flops 192 | bytes 1536 | tf_op jit(solution)/shard_map/psum | solution.py:38
  337.8 1.9 collective-permute-start.4
  339.7 0.7 gather_fusion.5
  340.4 0.9 gather_fusion.12
  341.3 1.3 multiply_subtract_fusion.1
  342.6 1.9 collective-permute-start.10
  344.5 0.9 gather_fusion.13
  345.6 8.0 %collective-permute-start.11 = (f32[64,4096]{1,0:T(8,128)S(1)}, f32[64,4096]{1,0:T(8,128)S(1)}, u32[]{:S(2)}, u32[]{:S(2)}) collective-permute-start(f32[64,4096]{1,0:T(8,128)S(1)} %broadcast_select_fusion.1), channel_id=1, source_target_pairs={{0,508},{4,0},{8,4},{12,8},{16,12},{20,16},{24,20},{28,24},{32,28}... | collective-permute-start | bytes 3145736 | tf_op jit(solution)/shard_map/ppermute | solution.py:24
  353.7 2.4 collective-permute-start.5
  356.2 10.3 %collective-permute-done.5 = f32[64,256]{1,0:T(8,128)S(1)} collective-permute-done((f32[64,256]{1,0:T(8,128)S(1)}, f32[64,256]{1,0:T(8,128)S(1)}, u32[]{:S(2)}, u32[]{:S(2)}) %collective-permute-start.5) | collective-permute-done | bytes 65568 | tf_op jit(solution)/shard_map/ppermute | solution.py:24
  367.4 11.8 %all-reduce = (f32[64]{0:T(128)S(1)}, f32[64]{0:T(128)S(1)}, f32[64]{0:T(128)S(1)}) all-reduce(f32[64]{0:T(128)S(1)} %get-tuple-element.17, f32[64]{0:T(128)S(1)} %get-tuple-element.11, f32[64]{0:T(128)S(1)} %get-tuple-element.10), channel_id=1, replica_groups=mesh['blk'=128,'rows'=4] {'rows'}, use_global_device_ids=true, to_apply=%region_25.27 | all-reduce | flops 192 | bytes 1536 | tf_op jit(solution)/shard_map/psum | solution.py:38
  379.4 0.7 gather_fusion.7
  380.2 0.8 copy.9
  380.9 0.9 gather_fusion.14
  381.9 1.6 multiply_add_fusion
  383.4 0.9 gather_fusion.15
  384.7 1.8 copy.10
  (67 shorter events, 5.0 us)
Async XLA Ops:
  12.3 14.3 %copy-start = (bf16[4096,128]{1,0:T(8,128)(2,1)S(1)}, bf16[4096,128]{1,0:T(8,128)(2,1)}, u32[]{:S(2)}) copy-start(bf16[4096,128]{1,0:T(8,128)(2,1)} %param.8) | copy-start | bytes 3145732
  12.3 200.4 %all-to-all-start = ((bf16[128,8,4096]{2,1,0:T(8,128)(2,1)}), bf16[128,8,4096]{2,1,0:T(8,128)(2,1)}, u32[]{:S(2)}, u32[]{:S(2)}) async-start(bf16[128,8,4096]{2,1,0:T(8,128)(2,1)} %stack.2), calls=%async_computation | async-start | bytes 16777216 | tf_op jit(solution)/shard_map/all_to_all | solution.py:12
  26.5 1.4 copy-start.2
  26.5 221.6 %reduce-scatter.2.cloned.1.call-start = ((), (), s32[]{:S(2)}) async-start(), calls=%async_computation.2 | async-start | bytes 655360 | tf_op jit(solution)/shard_map/reduce_scatter | solution.py:58
  262.9 37.4 %collective-permute-start.6 = (f32[64,4096]{1,0:T(8,128)}, f32[64,4096]{1,0:T(8,128)}, u32[]{:S(2)}, u32[]{:S(2)}) collective-permute-start(f32[64,4096]{1,0:T(8,128)} %get-tuple-element.49), channel_id=1, source_target_pairs={{0,4},{4,8},{8,12},{12,16},{16,20},{20,24},{24,28},{28,32},{32,36}... | collective-permute-start | bytes 3145736 | tf_op jit(solution)/shard_map/ppermute | solution.py:24
  265.8 8.1 %copy-start.1 = (f32[128,256]{1,0:T(8,128)S(1)}, f32[128,256]{1,0:T(8,128)}, u32[]{:S(2)}) copy-start(f32[128,256]{1,0:T(8,128)} %reduce-scatter.2.cloned.1.call-done) | copy-start | bytes 393220
  266.0 33.5 %collective-permute-start.7 = (f32[64,4096]{1,0:T(8,128)S(1)}, f32[64,4096]{1,0:T(8,128)S(1)}, u32[]{:S(2)}, u32[]{:S(2)}) collective-permute-start(f32[64,4096]{1,0:T(8,128)S(1)} %broadcast_select_fusion.3), channel_id=1, source_target_pairs={{0,508},{4,0},{8,4},{12,8},{16,12},{20,16},{24,20},{28,24},{32,28}... | collective-permute-start | bytes 3145736 | tf_op jit(solution)/shard_map/ppermute | solution.py:24
  274.0 13.5 %collective-permute-start = (f32[64,256]{1,0:T(8,128)S(1)}, f32[64,256]{1,0:T(8,128)S(1)}, u32[]{:S(2)}, u32[]{:S(2)}) collective-permute-start(f32[64,256]{1,0:T(8,128)S(1)} %get-tuple-element.57), channel_id=1, source_target_pairs={{0,4},{4,8},{8,12},{12,16},{16,20},{20,24},{24,28},{28,32},{32,36}... | collective-permute-start | bytes 196616 | tf_op jit(solution)/shard_map/ppermute | solution.py:24
  276.6 10.2 %collective-permute-start.1 = (f32[64,256]{1,0:T(8,128)S(1)}, f32[64,256]{1,0:T(8,128)S(1)}, u32[]{:S(2)}, u32[]{:S(2)}) collective-permute-start(f32[64,256]{1,0:T(8,128)S(1)} %broadcast_select_fusion.7), channel_id=1, source_target_pairs={{0,508},{4,0},{8,4},{12,8},{16,12},{20,16},{24,20},{28,24},{32,28}... | collective-permute-start | bytes 196616 | tf_op jit(solution)/shard_map/ppermute | solution.py:24
  302.9 38.3 %collective-permute-start.8 = (f32[64,4096]{1,0:T(8,128)}, f32[64,4096]{1,0:T(8,128)S(1)}, u32[]{:S(2)}, u32[]{:S(2)}) collective-permute-start(f32[64,4096]{1,0:T(8,128)} %get-tuple-element.55), channel_id=1, source_target_pairs={{0,4},{4,8},{8,12},{12,16},{16,20},{20,24},{24,28},{28,32},{32,36}... | collective-permute-start | bytes 3145736 | tf_op jit(solution)/shard_map/ppermute | solution.py:24
  306.9 33.4 %collective-permute-start.9 = (f32[64,4096]{1,0:T(8,128)}, f32[64,4096]{1,0:T(8,128)S(1)}, u32[]{:S(2)}, u32[]{:S(2)}) collective-permute-start(f32[64,4096]{1,0:T(8,128)} %broadcast_select_fusion.2), channel_id=1, source_target_pairs={{0,508},{4,0},{8,4},{12,8},{16,12},{20,16},{24,20},{28,24},{32,28}... | collective-permute-start | bytes 3145736 | tf_op jit(solution)/shard_map/ppermute | solution.py:24
  314.9 13.8 %collective-permute-start.2 = (f32[64,256]{1,0:T(8,128)S(1)}, f32[64,256]{1,0:T(8,128)S(1)}, u32[]{:S(2)}, u32[]{:S(2)}) collective-permute-start(f32[64,256]{1,0:T(8,128)S(1)} %get-tuple-element.63), channel_id=1, source_target_pairs={{0,4},{4,8},{8,12},{12,16},{16,20},{20,24},{24,28},{28,32},{32,36}... | collective-permute-start | bytes 196616 | tf_op jit(solution)/shard_map/ppermute | solution.py:24
  317.6 10.4 %collective-permute-start.3 = (f32[64,256]{1,0:T(8,128)S(1)}, f32[64,256]{1,0:T(8,128)S(1)}, u32[]{:S(2)}, u32[]{:S(2)}) collective-permute-start(f32[64,256]{1,0:T(8,128)S(1)} %broadcast_select_fusion.6), channel_id=1, source_target_pairs={{0,508},{4,0},{8,4},{12,8},{16,12},{20,16},{24,20},{28,24},{32,28}... | collective-permute-start | bytes 196616 | tf_op jit(solution)/shard_map/ppermute | solution.py:24
  337.8 29.4 %collective-permute-start.4 = (f32[64,256]{1,0:T(8,128)S(1)}, f32[64,256]{1,0:T(8,128)S(1)}, u32[]{:S(2)}, u32[]{:S(2)}) collective-permute-start(f32[64,256]{1,0:T(8,128)S(1)} %get-tuple-element.61), channel_id=1, source_target_pairs={{0,4},{4,8},{8,12},{12,16},{16,20},{20,24},{24,28},{28,32},{32,36}... | collective-permute-start | bytes 196616 | tf_op jit(solution)/shard_map/ppermute | solution.py:24
  342.6 39.2 %collective-permute-start.10 = (f32[64,4096]{1,0:T(8,128)}, f32[64,4096]{1,0:T(8,128)}, u32[]{:S(2)}, u32[]{:S(2)}) collective-permute-start(f32[64,4096]{1,0:T(8,128)} %get-tuple-element.53), channel_id=1, source_target_pairs={{0,4},{4,8},{8,12},{12,16},{16,20},{20,24},{24,28},{28,32},{32,36}... | collective-permute-start | bytes 3145736 | tf_op jit(solution)/shard_map/ppermute | solution.py:24
  345.6 35.3 %collective-permute-start.11 = (f32[64,4096]{1,0:T(8,128)S(1)}, f32[64,4096]{1,0:T(8,128)S(1)}, u32[]{:S(2)}, u32[]{:S(2)}) collective-permute-start(f32[64,4096]{1,0:T(8,128)S(1)} %broadcast_select_fusion.1), channel_id=1, source_target_pairs={{0,508},{4,0},{8,4},{12,8},{16,12},{20,16},{24,20},{28,24},{32,28}... | collective-permute-start | bytes 3145736 | tf_op jit(solution)/shard_map/ppermute | solution.py:24
  353.7 12.7 %collective-permute-start.5 = (f32[64,256]{1,0:T(8,128)S(1)}, f32[64,256]{1,0:T(8,128)S(1)}, u32[]{:S(2)}, u32[]{:S(2)}) collective-permute-start(f32[64,256]{1,0:T(8,128)S(1)} %broadcast_select_fusion.5), channel_id=1, source_target_pairs={{0,508},{4,0},{8,4},{12,8},{16,12},{20,16},{24,20},{28,24},{32,28}... | collective-permute-start | bytes 196616 | tf_op jit(solution)/shard_map/ppermute | solution.py:24
Sparse Core Ops, SparseCore 0:
  220.0 28.1 reduce-scatter.1
